TPU v7x, 32 devices: a whole 2x2x4 slice. The times are simulated.
32 devices in a mesh: dp: 4 (over y, x), expert: 8 (over z, core).
Axes of the slice: x: 2, y: 2, z: 4, core: 2. Of those that a mesh axis runs over, the one named last changes fastest.
Arguments:
- tokens: bfloat16 [1024, 4096], P('expert', 'dp'), may hold values from -6 to 6
- routes: int32 [1024, 4], P('expert'), may hold values from 0 to 7, all different within a row; in each aligned block of 128 rows (0 to 127, 128 to 255, ...) at most 128 rows name the same one
- route_weights: float32 [1024, 4], P('expert'), may hold values from 0.1 to 1
- gate_weight: bfloat16 [8, 4096, 1536], P('expert', None, 'dp'), may hold values from -0.09375 to 0.09375
- up_weight: bfloat16 [8, 4096, 1536], P('expert', None, 'dp'), may hold values from -0.09375 to 0.09375
- down_weight: bfloat16 [8, 1536, 4096], P('expert', 'dp'), may hold values from -0.15625 to 0.15625
- sketch_basis: bfloat16 [1536, 128], P('dp'), may hold values from -0.15625 to 0.15625
Outputs:
- mixed: bfloat16 [1024, 4096], P('expert', 'dp')
- sketch: float32 [8, 128, 1536], P('expert', None, 'dp')
Inputs may be any that keep to these rules, and one draw needn't show every extreme that they name: `routes`: each row names 4 different experts; within the rows of one device no expert is named more than 128 times, a bound that some block reaches.
All inputs are finite; a program needn't handle non-finite values.
Results may differ from a plain program's by a relative error of at most 0.017.
Values may be sent and summed in bfloat16 or wider, within the bound.
A program may use at most 128 MiB of HBM per device.

v0:
```python
import jax
import jax.numpy as jnp
from jax import lax
from jax.sharding import PartitionSpec as P

ridge_term = 1.0


def gram_matrix(factor_rows):
    return jnp.dot(factor_rows.T, factor_rows, precision=lax.Precision.HIGHEST)


def body(tokens, routes, route_weights, gate_weight, up_weight, down_weight, sketch_basis):
    owners = lax.axis_size("expert")
    token_count, route_count = routes.shape
    pair_count = token_count * route_count
    capacity = 2 * pair_count // owners
    slot_total = owners * capacity
    route_list = routes.reshape(-1)
    onehot = (route_list[:, None] == jnp.arange(owners, dtype=jnp.int32)[None, :]).astype(jnp.int32)
    before = jnp.cumsum(onehot, axis=0) - onehot
    slot_of = jnp.sum(before * onehot, axis=1)
    counts = jnp.sum(onehot, axis=0)
    target = route_list * capacity + slot_of
    source_pair = (
        jnp.zeros((slot_total,), jnp.int32).at[target].set(jnp.arange(pair_count, dtype=jnp.int32))
    )
    source_token = source_pair // route_count
    count_wire = counts.astype(jnp.bfloat16)
    features = lax.all_gather(tokens, "dp", axis=1, tiled=True)
    outgoing = features[source_token].reshape(owners, capacity, features.shape[1])
    arrived, arrived_counts = (
        lax.all_to_all(outgoing, "expert", split_axis=0, concat_axis=0, tiled=True),
        lax.all_to_all(count_wire, "expert", split_axis=0, concat_axis=0, tiled=True),
    )
    width = arrived.shape[2]
    live_count = arrived_counts.astype(jnp.int32)
    live_mask = (jnp.arange(capacity, dtype=jnp.int32)[None, :] < live_count[:, None]).reshape(-1)
    slot_rows = jnp.where(
        live_mask[:, None], arrived.reshape(slot_total, width), jnp.zeros((), jnp.bfloat16)
    )
    gate_local = gate_weight[0]
    up_local = up_weight[0]
    down_local = down_weight[0]
    gate_val = jnp.dot(slot_rows, gate_local, preferred_element_type=jnp.float32)
    up_val = jnp.dot(slot_rows, up_local, preferred_element_type=jnp.float32)
    hidden_block = (jax.nn.silu(gate_val) * up_val).astype(jnp.bfloat16)
    partial_value = jnp.dot(hidden_block, down_local, preferred_element_type=jnp.float32)
    sums = lax.psum_scatter(
        partial_value.reshape(owners, capacity, width).astype(jnp.bfloat16),
        "dp",
        scatter_dimension=2,
        tiled=True,
    )
    returned = lax.all_to_all(sums, "expert", split_axis=0, concat_axis=0, tiled=True)
    picked = returned.reshape(slot_total, returned.shape[2])[target]
    weighted = jnp.einsum(
        "tkd,tk->td",
        picked.reshape(token_count, route_count, returned.shape[2]).astype(jnp.float32),
        route_weights,
    )
    mixed = weighted.astype(jnp.bfloat16)
    sketch_part = jnp.dot(hidden_block, sketch_basis, preferred_element_type=jnp.float32)
    sketch_width = sketch_part.shape[1]
    eye_matrix = jnp.eye(sketch_width, dtype=jnp.float32)
    sketch_full = lax.psum(sketch_part.astype(jnp.bfloat16), "dp").astype(jnp.float32)
    lower_factor = jnp.linalg.cholesky(gram_matrix(sketch_full) + ridge_term * eye_matrix)
    projected = jnp.dot(
        sketch_full.T, hidden_block.astype(jnp.float32), precision=lax.Precision.HIGHEST
    )
    whitened = jax.scipy.linalg.solve_triangular(lower_factor, projected, lower=True)
    return (mixed, whitened[None])


def solution(mesh):
    return jax.shard_map(
        body,
        mesh=mesh,
        in_specs=(
            P("expert", "dp"),
            P("expert", None),
            P("expert", None),
            P("expert", None, "dp"),
            P("expert", None, "dp"),
            P("expert", "dp", None),
            P("dp", None),
        ),
        out_specs=(P("expert", "dp"), P("expert", None, "dp")),
        check_vma=False,
    )
```

profile of v0, /device:TPU:0, one launch (start us, length us, event | category | flops | bytes accessed | tf_op | source)
XLA Modules:
  0.0 452.7 jit_solution(8251671178967641806)
XLA Ops:
  7.2 0.0 copy-start
  7.2 0.0 all-gather.2.cloned.1.call-start
  7.2 0.7 all-gather.2.cloned.1.call-update
  7.9 1.0 copy.19
  8.9 0.1 eq.33
  9.0 0.1 eq.29
  9.1 1.1 reduce-window.6
  10.3 0.2 slice_reduce_fusion
  10.5 0.1 convert_reduce_fusion
  10.7 0.7 copy.20
  11.4 6.3 %all-to-all-start = ((bf16[8,1,1]{2,1,0:T(2,128)(2,1)}), bf16[8,1,1]{2,1,0:T(2,128)(2,1)S(1)}, u32[]{:S(2)}, u32[]{:S(2)}) async-start(bf16[8,1,1]{2,1,0:T(2,128)(2,1)} %copy.20), calls=%async_computation | async-start | bytes 8192 | tf_op jit(solution)/shard_map/all_to_all | solution.py:34
  17.7 0.7 broadcast_multiply_fusion
  18.4 0.1 copy.21
  18.5 0.1 mul.28
  18.6 2.4 scatter_custom_fusion
  21.1 18.1 %all-gather.2.cloned.1.call-done = bf16[128,4096]{1,0:T(8,128)(2,1)} async-done(((bf16[128,1024]{1,0:T(8,128)(2,1)}), bf16[128,4096]{1,0:T(8,128)(2,1)}) %all-gather.2.cloned.1.call-update) | async-done | bytes 1048592 | tf_op jit(solution)/shard_map/all_gather | solution.py:30
  39.2 16.4 %gather_fusion = bf16[1024,4096]{1,0:T(8,128)(2,1)} fusion(bf16[128,4096]{1,0:T(8,128)(2,1)} %all-gather.2.cloned.1.call-done, s32[1024]{0:T(1024)S(1)} %fusion.15), kind=kCustom, calls=%fused_computation | custom fusion | bytes 16781312 | tf_op jit(solution)/shard_map/gather | solution.py:31
  55.7 0.0 all-to-all-done
  55.7 5.0 %all-to-all-start.1 = ((bf16[8,128,4096]{2,1,0:T(8,128)(2,1)}), bf16[8,128,4096]{2,1,0:T(8,128)(2,1)}, u32[]{:S(2)}, u32[]{:S(2)}) async-start(bf16[8,128,4096]{2,1,0:T(8,128)(2,1)} %bitcast.53), calls=%async_computation.1 | async-start | bytes 16777216 | tf_op jit(solution)/shard_map/all_to_all | solution.py:33
  60.6 0.0 reduce-scatter.2.cloned.1.call-start
  60.7 0.2 convert_reduce_fusion.1
  60.9 0.1 iota_compare_fusion.5
  61.0 183.5 %all-to-all-done.1 = bf16[8,128,4096]{2,1,0:T(8,128)(2,1)} async-done(((bf16[8,128,4096]{2,1,0:T(8,128)(2,1)}), bf16[8,128,4096]{2,1,0:T(8,128)(2,1)}, u32[]{:S(2)}, u32[]{:S(2)}) %all-to-all-start.1) | async-done | bytes 8388640 | tf_op jit(solution)/shard_map/all_to_all | solution.py:33
  244.5 7.2 %broadcast_select_fusion = bf16[8,128,4096]{2,1,0:T(8,128)(2,1)} fusion(bf16[8,128,4096]{2,1,0:T(8,128)(2,1)} %all-to-all-done.1, pred[8,128]{1,0:T(8,128)(4,1)S(1)} %iota_compare_fusion.5), kind=kLoop, calls=%fused_computation.3 | loop fusion | flops 4194304 | bytes 16778240 | tf_op jit(solution)/shard_map/jit(_where)/select_n | solution.py:39
  251.7 0.0 copy-start.1
  251.8 0.0 copy-start.5
  251.8 8.0 %fusion.3 = f32[1024,384]{1,0:T(8,128)S(1)} fusion(bf16[1024,4096]{1,0:T(8,128)(2,1)} %bitcast.54, bf16[1,4096,384]{2,1,0:T(8,128)(2,1)} %param.10), kind=kOutput, calls=%fused_computation.8 | convolution fusion | flops 3221225472 | bytes 13107200 | tf_op jit(solution)/shard_map/dot_general | solution.py:45
  259.7 0.0 copy-done.1
  259.7 0.0 copy-done.5
  259.8 4.6 %multiply_convert_fusion = bf16[1024,384]{1,0:T(8,128)(2,1)S(1)} fusion(f32[1024,384]{1,0:T(8,128)S(1)} %fusion.3, bf16[1024,4096]{1,0:T(8,128)(2,1)S(1)} %bitcast.55, bf16[1,4096,384]{2,1,0:T(8,128)(2,1)S(1)} %copy-done.5), kind=kOutput, calls=%fused_computation.10 | convolution fusion | flops 3223584768 | bytes 13893632 | tf_op jit(solution)/shard_map/dot_general | solution.py:46
  264.3 0.0 copy-start.2
  264.3 0.9 copy-done.2
  265.2 0.0 copy-done
  265.2 6.6 %convolution_convert_fusion = bf16[8,128,4096]{2,1,0:T(8,128)(2,1)} fusion(bf16[8,128,384]{2,1,0:T(8,128)(2,1)S(1)} %bitcast.56, bf16[1,384,4096]{2,1,0:T(8,128)(2,1)S(1)} %copy-done), kind=kOutput, calls=%fused_computation.4 | convolution fusion | flops 3225419776 | bytes 12320768 | tf_op jit(solution)/shard_map/dot_general | solution.py:48
  271.9 0.0 reduce-scatter.2.cloned.1.call-update
  271.9 0.0 copy-start.3
  271.9 0.0 copy-start.4
  271.9 84.4 %reduce-scatter.2.cloned.1.call-done = bf16[8,128,1024]{2,1,0:T(8,128)(2,1)} async-done(((bf16[8,128,4096]{2,1,0:T(8,128)(2,1)}), bf16[8,128,1024]{2,1,0:T(8,128)(2,1)}) %reduce-scatter.2.cloned.1.call-update) | async-done | bytes 2097168 | tf_op jit(solution)/shard_map/reduce_scatter | solution.py:49
  356.3 4.6 %all-to-all-start.2 = ((bf16[8,128,1024]{2,1,0:T(8,128)(2,1)}), bf16[8,128,1024]{2,1,0:T(8,128)(2,1)}, u32[]{:S(2)}, u32[]{:S(2)}) async-start(bf16[8,128,1024]{2,1,0:T(8,128)(2,1)} %reduce-scatter.2.cloned.1.call-done), calls=%async_computation.3 | async-start | bytes 4194304 | tf_op jit(solution)/shard_map/all_to_all | solution.py:55
  360.9 0.2 all-reduce.2.cloned.1.call-start
  361.1 0.0 copy-done.3
  361.2 2.2 convolution_convert_fusion.1
  363.4 0.0 all-reduce.2.cloned.1.call-update
  363.4 0.0 copy-done.4
  363.4 0.2 copy.24
  363.6 45.4 %all-reduce.2.cloned.1.call-done = bf16[1024,128]{1,0:T(8,128)(2,1)} async-done(((bf16[1024,128]{1,0:T(8,128)(2,1)}), bf16[1024,128]{1,0:T(8,128)(2,1)}) %all-reduce.2.cloned.1.call-update) | async-done | bytes 262160 | tf_op jit(solution)/shard_map/psum | solution.py:66
  408.9 1.3 fusion.20
  410.2 0.1 copy.23
  410.4 11.7 %cholesky.17 = f32[128,128]{1,0:T(8,128)S(1)} custom-call(f32[128,128]{1,0:T(8,128)S(1)} %fusion.10), custom_call_target="Cholesky" | custom-call | tf_op jit(solution)/shard_map/jit(cholesky)/cholesky | solution.py:67
  422.1 0.6 compare_reduce_fusion
  422.8 0.7 fusion.7
  423.4 9.8 %custom-call.7 = f32[1,128,128]{1,2,0:T(8,128)S(1)} custom-call(f32[1,128,128]{2,1,0:T(8,128)S(1)} %fusion.7), custom_call_target="InvertDiagBlocksLowerTriangular" | custom-call | tf_op jit(solution)/shard_map/jit(_solve_triangular)/triangular_solve | solution.py:71
  433.2 1.5 fusion.21
  434.8 1.0 convolution_bitcast_fusion
  435.8 0.0 all-to-all-done.2
  435.8 5.3 %gather_fusion.1 = bf16[512,1024]{1,0:T(8,128)(2,1)} fusion(bf16[1024,1024]{1,0:T(8,128)(2,1)} %bitcast.12, s32[1024]{0:T(1024)S(1)} %pad_clamp_fusion), kind=kCustom, calls=%fused_computation.1 | custom fusion | bytes 2099200 | tf_op jit(solution)/shard_map/gather | solution.py:56
  441.2 2.3 reshape.115
  443.4 1.9 fusion.19
  445.4 0.8 copy.27
  (10 shorter events, 0.1 us)
Async XLA Ops:
  7.2 258.1 %copy-start = (bf16[1,384,4096]{2,1,0:T(8,128)(2,1)S(1)}, bf16[1,384,4096]{2,1,0:T(8,128)(2,1)}, u32[]{:S(2)}) copy-start(bf16[1,384,4096]{2,1,0:T(8,128)(2,1)} %param.12) | copy-start | bytes 9437188
  7.2 32.0 %all-gather.2.cloned.1.call-start = ((), (), s32[]{:S(2)}) async-start(), calls=%async_computation.4 | async-start | bytes 1310720 | tf_op jit(solution)/shard_map/all_gather | solution.py:30
  11.4 44.3 %all-to-all-start = ((bf16[8,1,1]{2,1,0:T(2,128)(2,1)}), bf16[8,1,1]{2,1,0:T(2,128)(2,1)S(1)}, u32[]{:S(2)}, u32[]{:S(2)}) async-start(bf16[8,1,1]{2,1,0:T(2,128)(2,1)} %copy.20), calls=%async_computation | async-start | bytes 8192 | tf_op jit(solution)/shard_map/all_to_all | solution.py:34
  55.7 188.9 %all-to-all-start.1 = ((bf16[8,128,4096]{2,1,0:T(8,128)(2,1)}), bf16[8,128,4096]{2,1,0:T(8,128)(2,1)}, u32[]{:S(2)}, u32[]{:S(2)}) async-start(bf16[8,128,4096]{2,1,0:T(8,128)(2,1)} %bitcast.53), calls=%async_computation.1 | async-start | bytes 16777216 | tf_op jit(solution)/shard_map/all_to_all | solution.py:33
  60.6 295.7 %reduce-scatter.2.cloned.1.call-start = ((), (), s32[]{:S(2)}) async-start(), calls=%async_computation.5 | async-start | bytes 10485760 | tf_op jit(solution)/shard_map/reduce_scatter | solution.py:49
  251.7 8.0 %copy-start.1 = (bf16[8,128,4096]{2,1,0:T(8,128)(2,1)S(1)}, bf16[8,128,4096]{2,1,0:T(8,128)(2,1)}, u32[]{:S(2)}) copy-start(bf16[8,128,4096]{2,1,0:T(8,128)(2,1)} %broadcast_select_fusion) | copy-start | bytes 25165828
  251.8 8.0 %copy-start.5 = (bf16[1,4096,384]{2,1,0:T(8,128)(2,1)S(1)}, bf16[1,4096,384]{2,1,0:T(8,128)(2,1)}, u32[]{:S(2)}) copy-start(bf16[1,4096,384]{2,1,0:T(8,128)(2,1)} %param.11) | copy-start | bytes 9437188
  264.3 0.9 copy-start.2
  271.9 89.3 %copy-start.3 = (bf16[384,128]{1,0:T(8,128)(2,1)S(1)}, bf16[384,128]{1,0:T(8,128)(2,1)}, u32[]{:S(2)}) copy-start(bf16[384,128]{1,0:T(8,128)(2,1)} %param.13) | copy-start | bytes 294916
  271.9 91.5 %copy-start.4 = (f32[128,4]{0,1:T(4,128)S(1)}, f32[128,4]{0,1:T(4,128)}, u32[]{:S(2)}) copy-start(f32[128,4]{0,1:T(4,128)} %param.9) | copy-start | bytes 6148
  356.3 79.5 %all-to-all-start.2 = ((bf16[8,128,1024]{2,1,0:T(8,128)(2,1)}), bf16[8,128,1024]{2,1,0:T(8,128)(2,1)}, u32[]{:S(2)}, u32[]{:S(2)}) async-start(bf16[8,128,1024]{2,1,0:T(8,128)(2,1)} %reduce-scatter.2.cloned.1.call-done), calls=%async_computation.3 | async-start | bytes 4194304 | tf_op jit(solution)/shard_map/all_to_all | solution.py:55
  360.9 48.0 %all-reduce.2.cloned.1.call-start = ((), (), s32[]{:S(2)}) async-start(), calls=%async_computation.6 | async-start | bytes 524288 | tf_op jit(solution)/shard_map/psum | solution.py:66
Sparse Core Ops, SparseCore 0:
  9.9 29.3 all-gather.1
  272.0 84.2 reduce-scatter.1
  365.5 43.3 all-reduce.1
where the time goes:
time: 453 us
  waiting for transfers between devices  332 us (73%)
  other arithmetic  32.5 us (7%)
  local copies, waits for them, and re-layouts  30.8 us (7%)
  matrix products  27.2 us (6%)
  starting transfers between devices  16.2 us (4%)
  between operations  14 us (3%)
    all_to_all x1, waiting for transfers between devices, body(): lax.all_to_all(outgoing, 'expert', split_axis=0, concat_axis=0, tiled=True)  184 us
    reduce_scatter x1, waiting for transfers between devices, body(): lax.psum_scatter(partial_value.reshape(owners, capacity, width).astype(jn...  84.4 us
    psum x1, waiting for transfers between devices, body(): lax.psum(sketch_part.astype(jnp.bfloat16), 'dp').astype(jnp.float32)  45.4 us
    all_gather x1, waiting for transfers between devices, body(): features = lax.all_gather(tokens, 'dp', axis=1, tiled=True)  18.1 us
    gather x1, local copies, waits for them, and re-layouts, body(): features[source_token].reshape(owners, capacity, features.shape[1])  16.4 us
    another operation x3, other arithmetic, body(): jnp.linalg.cholesky(gram_matrix(sketch_full) + ridge_term * eye_matrix)  12.4 us
    another operation x2, other arithmetic, body(): jax.scipy.linalg.solve_triangular(lower_factor, projected, lower=True)  10.5 us
  transfers between devices with their start and end apart: 6, of which 4 were waited for; matrix products, arithmetic and copies ran while one was open for 12% of the time, Pallas kernels for 0%

commit v1 on v0

--- a/solution.py
+++ b/solution.py
@@ -1,7 +1,12 @@
 import jax
 import jax.numpy as jnp
 from jax import lax
+from jax.experimental import pallas as pl
+from jax.experimental.pallas import tpu as pltpu
 from jax.sharding import PartitionSpec as P
+
+MESH = pl.DeviceIdType.MESH
+VMEM_BYTES = 56 * 1024 * 1024
 
 ridge_term = 1.0
 
@@ -72,9 +77,279 @@
     return (mixed, whitened[None])
 
 
+def place():
+    dp, expert = lax.axis_index("dp"), lax.axis_index("expert")
+    y, x = dp // 2, dp % 2
+    z, core = expert // 2, expert % 2
+    return dp, expert, y, x, z, core
+
+
+def enter(partners):
+    barrier = pltpu.get_barrier_semaphore()
+    for partner in partners:
+        pl.semaphore_signal(barrier, inc=1, device_id=partner, device_id_type=MESH)
+    pl.semaphore_wait(barrier, len(partners))
+
+
+def gather_kernel(tok_ref, out_ref, own_sem, z_send, z_recv, x_send, x_recv, y_send, y_recv, dx_send, dx_recv, dy_send, dy_recv, s_send, s_recv):
+    dp, expert, y, x, z, core = place()
+    rows, cols = tok_ref.shape
+    half = rows // 2
+    x_dp, y_dp, d_dp = y * 2 + 1 - x, (1 - y) * 2 + x, (1 - y) * 2 + 1 - x
+    other = (dp, z * 2 + 1 - core)
+    x_dev, y_dev = (x_dp, expert), (y_dp, expert)
+    z_devs = [(dp, (z + k) % 4 * 2 + core) for k in range(1, 4)]
+    enter([other, x_dev, y_dev] + z_devs)
+
+    def block(dp_at, k, low=0, count=rows):
+        at = ((z + 4 - k) % 4 * 2 + core) * rows + low
+        return out_ref.at[pl.ds(at, count), pl.ds(dp_at * cols, cols)]
+
+    def copy(ref, dst, send, recv, device):
+        return pltpu.make_async_remote_copy(
+            src_ref=ref, dst_ref=dst, send_sem=send, recv_sem=recv, device_id=device, device_id_type=MESH
+        )
+
+    sent = []
+
+    def go(*args):
+        c = copy(*args)
+        c.start()
+        sent.append(c)
+
+    def arrived(dst, send, recv):
+        copy(dst, dst, send, recv, other).wait_recv()
+
+    own = pltpu.make_async_copy(tok_ref, block(dp, 0), own_sem)
+    own.start()
+    go(tok_ref, block(dp, 0), x_send.at[0], x_recv.at[0], x_dev)
+    go(tok_ref, block(dp, 0), y_send.at[0], y_recv.at[0], y_dev)
+    for k in range(1, 4):
+        go(tok_ref, block(dp, 0), z_send.at[k - 1], z_recv.at[k - 1], z_devs[k - 1])
+    go(tok_ref, block(dp, 0), s_send.at[0], s_recv.at[0], other)
+
+    def near(k):
+        arrived(block(x_dp, k), x_send.at[k], x_recv.at[k])
+        go(block(x_dp, k, 0, half), block(x_dp, k, 0, half), dy_send.at[k], dy_recv.at[k], y_dev)
+        go(block(x_dp, k), block(x_dp, k), s_send.at[4 + k], s_recv.at[4 + k], other)
+        arrived(block(y_dp, k), y_send.at[k], y_recv.at[k])
+        go(block(y_dp, k, half, half), block(y_dp, k, half, half), dx_send.at[k], dx_recv.at[k], x_dev)
+        go(block(y_dp, k), block(y_dp, k), s_send.at[8 + k], s_recv.at[8 + k], other)
+
+    def far(k):
+        arrived(block(d_dp, k, 0, half), dy_send.at[k], dy_recv.at[k])
+        arrived(block(d_dp, k, half, half), dx_send.at[k], dx_recv.at[k])
+        go(block(d_dp, k), block(d_dp, k), s_send.at[12 + k], s_recv.at[12 + k], other)
+
+    def column(k):
+        arrived(block(dp, k), z_send.at[k - 1], z_recv.at[k - 1])
+        go(block(dp, k), block(dp, k), x_send.at[k], x_recv.at[k], x_dev)
+        go(block(dp, k), block(dp, k), y_send.at[k], y_recv.at[k], y_dev)
+        go(block(dp, k), block(dp, k), s_send.at[k], s_recv.at[k], other)
+
+    column(1)
+    near(0)
+    column(3)
+    column(2)
+    near(1)
+    far(0)
+    near(3)
+    far(1)
+    near(2)
+    far(3)
+    far(2)
+    for j, dp_at in enumerate((dp, x_dp, y_dp, d_dp)):
+        for k in range(4):
+            at = ((z + 4 - k) % 4 * 2 + 1 - core) * rows
+            dst = out_ref.at[pl.ds(at, rows), pl.ds(dp_at * cols, cols)]
+            arrived(dst, s_send.at[4 * j + k], s_recv.at[4 * j + k])
+    own.wait()
+    for c in sent:
+        c.wait_send()
+
+
+def gather_tokens(tokens):
+    rows, cols = tokens.shape
+    dma = pltpu.SemaphoreType.DMA
+    return pl.pallas_call(
+        gather_kernel,
+        out_shape=jax.ShapeDtypeStruct((rows * 8, cols * 4), tokens.dtype),
+        in_specs=[pl.BlockSpec(memory_space=pl.ANY)],
+        out_specs=pl.BlockSpec(memory_space=pl.ANY),
+        scratch_shapes=[dma, dma((3,)), dma((3,))] + [dma((4,))] * 8 + [dma((16,))] * 2,
+        compiler_params=pltpu.CompilerParams(collective_id=0, has_side_effects=True, vmem_limit_bytes=VMEM_BYTES),
+    )(tokens)
+
+
+def combine_kernel(hid_ref, down_ref, basis_ref, w_ref, out_ref, zfull_ref, sbuf, rbuf, pbuf, dxb, dyb, xb, yb, zb, zr, zs, zn, z2, zz,
+                   s_send, s_recv, dx_send, dx_recv, dy_send, dy_recv, x_send, x_recv, y_send, y_recv, z_send, z_recv, q_send, q_recv):
+    dp, expert, y, x, z, core = place()
+    rows, cols = out_ref.shape
+    half = rows // 2
+    x_dp, y_dp, d_dp = y * 2 + 1 - x, (1 - y) * 2 + x, (1 - y) * 2 + 1 - x
+    targets = (dp, x_dp, y_dp, d_dp)
+    other = (dp, z * 2 + 1 - core)
+    x_dev, y_dev = (x_dp, expert), (y_dp, expert)
+    z_devs = [(dp, (z + k) % 4 * 2 + core) for k in range(1, 4)]
+    enter([other, x_dev, y_dev] + z_devs)
+
+    def copy(ref, dst, send, recv, device):
+        return pltpu.make_async_remote_copy(
+            src_ref=ref, dst_ref=dst, send_sem=send, recv_sem=recv, device_id=device, device_id_type=MESH
+        )
+
+    def q_copy(i, ref, dst, device):
+        return copy(ref, dst, q_send.at[i], q_recv.at[i], device)
+
+    count = zs.shape[0] // 2
+    lo, hi = pl.ds(0, count), pl.ds(count, count)
+    zs[...] = jnp.dot(hid_ref[...], basis_ref[...], preferred_element_type=jnp.float32).astype(zs.dtype)
+    q = [
+        q_copy(0, zs.at[lo], zn.at[lo], x_dev),
+        q_copy(1, zs.at[hi], zn.at[hi], y_dev),
+        q_copy(2, z2.at[lo], zz.at[lo], y_dev),
+        q_copy(3, z2.at[hi], zz.at[hi], x_dev),
+    ]
+    q[0].start()
+    q[1].start()
+
+    def product(k, j, side):
+        at = pl.multiple_of(((z + k) % 4 * 2 + side) * rows, rows)
+        col = pl.multiple_of(targets[j] * cols, cols)
+        dot = jnp.dot(hid_ref[pl.ds(at, rows), :], down_ref[:, pl.ds(col, cols)], preferred_element_type=jnp.float32)
+        return dot * w_ref[pl.ds(at, rows), :]
+
+    def s_copy(k, j):
+        return copy(sbuf.at[k, j], rbuf.at[k, j], s_send.at[k, j], s_recv.at[k, j], other)
+
+    def dx_copy(k):
+        return copy(pbuf.at[k, 3, pl.ds(0, half)], dxb.at[k], dx_send.at[k], dx_recv.at[k], x_dev)
+
+    def dy_copy(k):
+        return copy(pbuf.at[k, 3, pl.ds(half, half)], dyb.at[k], dy_send.at[k], dy_recv.at[k], y_dev)
+
+    def x_copy(k):
+        return copy(pbuf.at[k, 1], xb.at[k], x_send.at[k], x_recv.at[k], x_dev)
+
+    def y_copy(k):
+        return copy(pbuf.at[k, 2], yb.at[k], y_send.at[k], y_recv.at[k], y_dev)
+
+    def z_copy(k):
+        return copy(zb.at[k - 1], zr.at[k - 1], z_send.at[k - 1], z_recv.at[k - 1], z_devs[k - 1])
+
+    order = (2, 1, 3, 0)
+    for k in order:
+        for j in (3, 1, 2, 0):
+            sbuf[k, j] = product(k, j, 1 - core).astype(sbuf.dtype)
+            s_copy(k, j).start()
+    for i, part in ((0, lo), (1, hi)):
+        q[i].wait_recv()
+        z2[part, :] = (zs[part, :].astype(jnp.float32) + zn[part, :].astype(jnp.float32)).astype(z2.dtype)
+        q[2 + i].start()
+
+    def own(k, j):
+        mine = product(k, j, core)
+        s_copy(k, j).wait_recv()
+        pbuf[k, j] = (mine + rbuf[k, j].astype(jnp.float32)).astype(pbuf.dtype)
+
+    def first(k):
+        own(k, 3)
+        dx_copy(k).start()
+        dy_copy(k).start()
+        own(k, 1)
+        own(k, 2)
+        own(k, 0)
+
+    def second(k):
+        dx_copy(k).wait_recv()
+        pbuf[k, 2, 0:half] = (pbuf[k, 2, 0:half].astype(jnp.float32) + dxb[k].astype(jnp.float32)).astype(pbuf.dtype)
+        y_copy(k).start()
+        dy_copy(k).wait_recv()
+        pbuf[k, 1, half:rows] = (pbuf[k, 1, half:rows].astype(jnp.float32) + dyb[k].astype(jnp.float32)).astype(pbuf.dtype)
+        x_copy(k).start()
+
+    def third(k):
+        x_copy(k).wait_recv()
+        y_copy(k).wait_recv()
+        return pbuf[k, 0].astype(jnp.float32) + xb[k].astype(jnp.float32) + yb[k].astype(jnp.float32)
+
+    def fourth(k):
+        zb[k - 1] = third(k).astype(zb.dtype)
+        z_copy(k).start()
+
+    for k in order:
+        first(k)
+    q[2].wait_recv()
+    q[3].wait_recv()
+    zfull_ref[...] = (z2[...].astype(jnp.float32) + zz[...].astype(jnp.float32)).astype(zfull_ref.dtype)
+    second(2)
+    second(1)
+    second(3)
+    fourth(2)
+    second(0)
+    fourth(1)
+    fourth(3)
+    total = third(0)
+    for k in (2, 1, 3):
+        z_copy(k).wait_recv()
+        total = total + zr[k - 1].astype(jnp.float32)
+    out_ref[...] = total.astype(out_ref.dtype)
+    for c in q:
+        c.wait_send()
+    for k in range(4):
+        for j in range(4):
+            s_copy(k, j).wait_send()
+        for c in (dx_copy, dy_copy, x_copy, y_copy):
+            c(k).wait_send()
+        if k:
+            z_copy(k).wait_send()
+
+
+def combine(hidden, down, basis, weight, rows, cols):
+    total, sk = hidden.shape[0], basis.shape[1]
+    dma, vmem, kind = pltpu.SemaphoreType.DMA, pltpu.VMEM, jnp.bfloat16
+    spec = pl.BlockSpec(memory_space=pltpu.VMEM)
+    return pl.pallas_call(
+        combine_kernel,
+        out_shape=(jax.ShapeDtypeStruct((rows, cols), kind), jax.ShapeDtypeStruct((total, sk), kind)),
+        in_specs=[spec] * 4,
+        out_specs=(spec, spec),
+        scratch_shapes=[vmem((4, 4, rows, cols), kind)] * 3
+        + [vmem((4, rows // 2, cols), kind)] * 2
+        + [vmem((4, rows, cols), kind)] * 2
+        + [vmem((3, rows, cols), kind)] * 2
+        + [vmem((total, sk), kind)] * 4
+        + [dma((4, 4))] * 2
+        + [dma((4,))] * 8
+        + [dma((3,))] * 2
+        + [dma((4,))] * 2,
+        compiler_params=pltpu.CompilerParams(collective_id=1, has_side_effects=True, vmem_limit_bytes=VMEM_BYTES),
+    )(hidden, down, basis, weight)
+
+
+def dense_body(tokens, routes, route_weights, gate_weight, up_weight, down_weight, sketch_basis):
+    owners = lax.axis_size("expert")
+    experts = jnp.arange(owners, dtype=jnp.int32)
+    table = jnp.sum(jnp.where(routes[:, :, None] == experts, route_weights[:, :, None], 0.0), axis=1)
+    tables = lax.all_gather(table, "expert", axis=0, tiled=True)
+    features = gather_tokens(tokens)
+    weight = jnp.sum(jnp.where(experts == lax.axis_index("expert"), tables, 0.0), axis=1, keepdims=True)
+    gate_val = jnp.dot(features, gate_weight[0], preferred_element_type=jnp.float32)
+    up_val = jnp.dot(features, up_weight[0], preferred_element_type=jnp.float32)
+    hidden = jnp.where(weight > 0, jax.nn.silu(gate_val) * up_val, 0.0).astype(jnp.bfloat16)
+    mixed, sketch_full = combine(hidden, down_weight[0], sketch_basis, weight, *tokens.shape)
+    contract = (((0,), (0,)), ((), ()))
+    gram = lax.dot_general(sketch_full, sketch_full, contract, preferred_element_type=jnp.float32)
+    lower_factor = jnp.linalg.cholesky(gram + ridge_term * jnp.eye(gram.shape[0], dtype=jnp.float32))
+    projected = lax.dot_general(sketch_full, hidden, contract, preferred_element_type=jnp.float32)
+    whitened = jax.scipy.linalg.solve_triangular(lower_factor, projected, lower=True)
+    return (mixed, whitened[None])
+
+
 def solution(mesh):
+    dense = mesh.shape["dp"] == 4 and mesh.shape["expert"] == 8
     return jax.shard_map(
-        body,
+        dense_body if dense else body,
         mesh=mesh,
         in_specs=(
             P("expert", "dp"),

time: 453 us -> 172 us (0.38)
  waiting for transfers between devices: 332 us -> 0 us
  Pallas kernels: 0 us -> 103 us
  local copies, waits for them, and re-layouts: 30.8 us -> 2.8 us
  blocking collectives: 0 us -> 20.6 us
  starting transfers between devices: 16.2 us -> 0 us
  between operations: 14 us -> 0.74 us
  other arithmetic: 32.5 us -> 23 us
  matrix products: 27.2 us -> 22.2 us
    all_to_all x3 -> x0, waiting for transfers between devices: 184 us -> none  [the longest x1 184 us: body(): lax.all_to_all(outgoing, 'expert', split_axis=0, concat_axis=0, tiled=True)]
    pallas_call x0 -> x2, Pallas kernels: none -> 103 us  [the longest x1 56.8 us: combine(): pl.pallas_call(combine_kernel, out_shape=(jax.ShapeDtypeStruct((rows, col...]
    reduce_scatter x1 -> x0, waiting for transfers between devices: 84.4 us -> none  [body(): lax.psum_scatter(partial_value.reshape(owners, capacity, width).astype(jn...]
    psum x1 -> x0, waiting for transfers between devices: 45.4 us -> none  [body(): lax.psum(sketch_part.astype(jnp.bfloat16), 'dp').astype(jnp.float32)]
    gather x2 -> x0, local copies, waits for them, and re-layouts: 21.8 us -> none  [the longest x1 16.4 us: body(): features[source_token].reshape(owners, capacity, features.shape[1])]
    all_gather x0 -> x1, blocking collectives: none -> 20.6 us  [dense_body(): tables = lax.all_gather(table, 'expert', axis=0, tiled=True)]
    all_gather x1 -> x0, waiting for transfers between devices: 18.1 us -> none  [body(): features = lax.all_gather(tokens, 'dp', axis=1, tiled=True)]
    all_to_all x3 -> x0, starting transfers between devices: 15.9 us -> none  [the longest x1 6.33 us: body(): lax.all_to_all(count_wire, 'expert', split_axis=0, concat_axis=0, tiled=T...]
  transfers between devices with their start and end apart: 6 -> 0, of which waited for: 4 -> 0; matrix products, arithmetic and copies ran while one was open for 12% -> 0% of each run, Pallas kernels for 0% -> 0%
where the time goes in v1:
time: 172 us
  Pallas kernels  103 us (60%)
  other arithmetic  23 us (13%)
  matrix products  22.2 us (13%)
  blocking collectives  20.6 us (12%)
  local copies, waits for them, and re-layouts  2.8 us (2%)
    pallas_call x1, Pallas kernels, combine(): pl.pallas_call(combine_kernel, out_shape=(jax.ShapeDtypeStruct((rows, col...  56.8 us
    pallas_call x1, Pallas kernels, gather_tokens(): pl.pallas_call(gather_kernel, out_shape=jax.ShapeDtypeStruct((rows * 8, c...  45.7 us
    all_gather x1, blocking collectives, dense_body(): tables = lax.all_gather(table, 'expert', axis=0, tiled=True)  20.6 us
    another operation x3, other arithmetic, dense_body(): jnp.linalg.cholesky(gram + ridge_term * jnp.eye(gram.shape[0], dtype=jnp....  12.4 us
    another operation x2, other arithmetic, dense_body(): jax.scipy.linalg.solve_triangular(lower_factor, projected, lower=True)  10.5 us
    dot_general x1, matrix products, dense_body(): up_val = jnp.dot(features, up_weight[0], preferred_element_type=jnp.float32)  10.2 us
    dot_general x1, matrix products, dense_body(): jnp.dot(features, gate_weight[0], preferred_element_type=jnp.float32)  8.1 us

profile of v1, /device:TPU:0, one launch (start us, length us, event | category | flops | bytes accessed | tf_op | source)
XLA Modules:
  0.0 171.9 jit_solution(12952498584791374264)
XLA Ops:
  0.6 0.0 copy-start
  0.6 45.7 %shard_map.86 = bf16[1024,4096]{1,0:T(8,128)(2,1)} custom-call(bf16[128,1024]{1,0:T(8,128)(2,1)} %tok_ref.1), custom_call_target="tpu_custom_call" | custom-call | tf_op jit(solution)/shard_map/pallas_call | solution.py:174
  46.4 0.0 copy-done
  46.4 0.0 copy-start.1
  46.4 0.0 copy-start.2
  46.4 8.1 %fusion.2 = f32[1024,384]{1,0:T(8,128)} fusion(bf16[1024,4096]{1,0:T(8,128)(2,1)} %shard_map.86, bf16[1,4096,384]{2,1,0:T(8,128)(2,1)S(1)} %copy-done), kind=kOutput, calls=%fused_computation.2 | convolution fusion | flops 3221225472 | bytes 13107200 | tf_op jit(solution)/shard_map/dot_general | solution.py:337
  54.5 0.0 copy-done.1
  54.5 0.0 copy-done.2
  54.5 20.6 %all_gather.3 = f32[1024,8]{0,1:T(8,128)S(1)} all-gather(f32[128,8]{0,1:T(8,128)S(1)} %select_reduce_fusion.2), channel_id=1, replica_groups=mesh['dp'=4,'expert'=8] {'expert'}, dimensions={0}, use_global_device_ids=true | all-gather | bytes 36864 | tf_op jit(solution)/shard_map/all_gather | solution.py:334
  75.1 0.1 select_reduce_fusion.1
  75.2 10.2 %select_convert_fusion.hid_ref = bf16[1024,384]{1,0:T(8,128)(2,1)} fusion(f32[1024,384]{1,0:T(8,128)} %fusion.2, bf16[1024,4096]{1,0:T(8,128)(2,1)} %shard_map.86, bf16[1,4096,384]{2,1,0:T(8,128)(2,1)} %param.11, pred[1024]{0:T(1024)(128)(4,1)S(1)} %broadcast_compare_fusion), kind=kOutput, calls=%fused_computation.4 | convolution fusion | flops 3223977984 | bytes 13894656 | tf_op jit(solution)/shard_map/dot_general | solution.py:338
  85.4 1.0 copy.16.w_ref
  86.5 56.8 %shard_map.87 = (bf16[128,1024]{1,0:T(8,128)(2,1)}, bf16[1024,128]{1,0:T(8,128)(2,1)}) custom-call(bf16[1024,384]{1,0:T(8,128)(2,1)} %select_convert_fusion.hid_ref, bf16[384,4096]{1,0:T(8,128)(2,1)} %bitcast.30, bf16[384,128]{1,0:T(8,128)(2,1)} %basis_ref.1, f32[1024,1]{1,0:T(8,128)} %copy.16.w_ref), custom_call_target="tpu_custom_call" | custom-call | tf_op jit(solution)/shard_map/pallas_call | solution.py:312
  143.3 1.3 fusion.10
  144.6 0.1 copy.17
  144.7 11.7 %cholesky.17 = f32[128,128]{1,0:T(8,128)S(1)} custom-call(f32[128,128]{1,0:T(8,128)S(1)} %fusion.9), custom_call_target="Cholesky" | custom-call | tf_op jit(solution)/shard_map/jit(cholesky)/cholesky | solution.py:343
  156.5 0.6 compare_reduce_fusion
  157.1 0.7 fusion.6
  157.8 9.8 %custom-call.7 = f32[1,128,128]{1,2,0:T(8,128)S(1)} custom-call(f32[1,128,128]{2,1,0:T(8,128)S(1)} %fusion.6), custom_call_target="InvertDiagBlocksLowerTriangular" | custom-call | tf_op jit(solution)/shard_map/jit(_solve_triangular)/triangular_solve | solution.py:345
  167.6 1.5 fusion.11
  169.2 1.0 convolution_bitcast_fusion
  170.2 1.7 copy.19
  (5 shorter events, 0.1 us)
Async XLA Ops:
  0.6 45.8 %copy-start = (bf16[1,4096,384]{2,1,0:T(8,128)(2,1)S(1)}, bf16[1,4096,384]{2,1,0:T(8,128)(2,1)}, u32[]{:S(2)}) copy-start(bf16[1,4096,384]{2,1,0:T(8,128)(2,1)} %param.10) | copy-start | bytes 9437188
  46.4 8.1 %copy-start.1 = (f32[128,4]{0,1:T(4,128)S(1)}, f32[128,4]{0,1:T(4,128)}, u32[]{:S(2)}) copy-start(f32[128,4]{0,1:T(4,128)} %param.9) | copy-start | bytes 6148
  46.4 8.1 %copy-start.2 = (s32[128,4]{0,1:T(4,128)S(1)}, s32[128,4]{0,1:T(4,128)}, u32[]{:S(2)}) copy-start(s32[128,4]{0,1:T(4,128)} %param.8) | copy-start | bytes 6148

commit v2 on v1

--- a/solution.py
+++ b/solution.py
@@ -91,7 +91,7 @@
     pl.semaphore_wait(barrier, len(partners))
 
 
-def gather_kernel(tok_ref, out_ref, own_sem, z_send, z_recv, x_send, x_recv, y_send, y_recv, dx_send, dx_recv, dy_send, dy_recv, s_send, s_recv):
+def gather_kernel(tok_ref, tab_ref, out_ref, tabs_ref, own_sem, tab_sem, t_send, t_recv, z_send, z_recv, x_send, x_recv, y_send, y_recv, dx_send, dx_recv, dy_send, dy_recv, s_send, s_recv):
     dp, expert, y, x, z, core = place()
     rows, cols = tok_ref.shape
     half = rows // 2
@@ -99,7 +99,8 @@
     other = (dp, z * 2 + 1 - core)
     x_dev, y_dev = (x_dp, expert), (y_dp, expert)
     z_devs = [(dp, (z + k) % 4 * 2 + core) for k in range(1, 4)]
-    enter([other, x_dev, y_dev] + z_devs)
+    cross = [(dp, (z + k) % 4 * 2 + 1 - core) for k in range(1, 4)]
+    enter([other, x_dev, y_dev] + z_devs + cross)
 
     def block(dp_at, k, low=0, count=rows):
         at = ((z + 4 - k) % 4 * 2 + core) * rows + low
@@ -122,11 +123,19 @@
 
     own = pltpu.make_async_copy(tok_ref, block(dp, 0), own_sem)
     own.start()
+
+    def table_at(k, side):
+        return tabs_ref.at[pl.ds(((z + 4 - k) % 4 * 2 + side) * rows, rows), :]
+
+    own_tab = pltpu.make_async_copy(tab_ref, table_at(0, core), tab_sem)
+    own_tab.start()
     go(tok_ref, block(dp, 0), x_send.at[0], x_recv.at[0], x_dev)
     go(tok_ref, block(dp, 0), y_send.at[0], y_recv.at[0], y_dev)
     for k in range(1, 4):
         go(tok_ref, block(dp, 0), z_send.at[k - 1], z_recv.at[k - 1], z_devs[k - 1])
     go(tok_ref, block(dp, 0), s_send.at[0], s_recv.at[0], other)
+    for i, device in enumerate([other] + z_devs + cross):
+        go(tab_ref, table_at(0, core), t_send.at[i], t_recv.at[i], device)
 
     def near(k):
         arrived(block(x_dp, k), x_send.at[k], x_recv.at[k])
@@ -163,25 +172,32 @@
             at = ((z + 4 - k) % 4 * 2 + 1 - core) * rows
             dst = out_ref.at[pl.ds(at, rows), pl.ds(dp_at * cols, cols)]
             arrived(dst, s_send.at[4 * j + k], s_recv.at[4 * j + k])
+    for i in range(7):
+        k, side = (0, 1 - core) if i == 0 else (i, core) if i < 4 else (i - 3, 1 - core)
+        arrived(table_at(k, side), t_send.at[i], t_recv.at[i])
     own.wait()
+    own_tab.wait()
     for c in sent:
         c.wait_send()
 
 
-def gather_tokens(tokens):
+def gather_tokens(tokens, table):
     rows, cols = tokens.shape
     dma = pltpu.SemaphoreType.DMA
     return pl.pallas_call(
         gather_kernel,
-        out_shape=jax.ShapeDtypeStruct((rows * 8, cols * 4), tokens.dtype),
-        in_specs=[pl.BlockSpec(memory_space=pl.ANY)],
-        out_specs=pl.BlockSpec(memory_space=pl.ANY),
-        scratch_shapes=[dma, dma((3,)), dma((3,))] + [dma((4,))] * 8 + [dma((16,))] * 2,
+        out_shape=(
+            jax.ShapeDtypeStruct((rows * 8, cols * 4), tokens.dtype),
+            jax.ShapeDtypeStruct((rows * 8, table.shape[1]), table.dtype),
+        ),
+        in_specs=[pl.BlockSpec(memory_space=pl.ANY)] * 2,
+        out_specs=(pl.BlockSpec(memory_space=pl.ANY),) * 2,
+        scratch_shapes=[dma, dma, dma((7,)), dma((7,)), dma((3,)), dma((3,))] + [dma((4,))] * 8 + [dma((16,))] * 2,
         compiler_params=pltpu.CompilerParams(collective_id=0, has_side_effects=True, vmem_limit_bytes=VMEM_BYTES),
-    )(tokens)
-
-
-def combine_kernel(hid_ref, down_ref, basis_ref, w_ref, out_ref, zfull_ref, sbuf, rbuf, pbuf, dxb, dyb, xb, yb, zb, zr, zs, zn, z2, zz,
+    )(tokens, table)
+
+
+def combine_kernel(hid_ref, down_ref, basis_ref, w_ref, out_ref, sketch_ref, work, sbuf, rbuf, pbuf, dxb, dyb, xb, yb, zb, zr, zs, zn, z2, zz,
                    s_send, s_recv, dx_send, dx_recv, dy_send, dy_recv, x_send, x_recv, y_send, y_recv, z_send, z_recv, q_send, q_recv):
     dp, expert, y, x, z, core = place()
     rows, cols = out_ref.shape
@@ -281,20 +297,61 @@
         first(k)
     q[2].wait_recv()
     q[3].wait_recv()
-    zfull_ref[...] = (z2[...].astype(jnp.float32) + zz[...].astype(jnp.float32)).astype(zfull_ref.dtype)
+    q[0].wait_send()
+    q[1].wait_send()
+    zs[...] = (z2[...].astype(jnp.float32) + zz[...].astype(jnp.float32)).astype(zs.dtype)
     second(2)
     second(1)
     second(3)
+    second(0)
+    sk = work.shape[0]
+    panel_rows = 32
+    contract = (((0,), (0,)), ((), ()))
+    line = lax.broadcasted_iota(jnp.int32, (sk, sk), 0)
+    eye = (line == lax.broadcasted_iota(jnp.int32, (sk, sk), 1)).astype(jnp.float32)
+    work[:, 0:sk] = lax.dot_general(zs[...], zs[...], contract, preferred_element_type=jnp.float32) + ridge_term * eye
+    work[:, sk:] = eye
+
+    def eliminate(p):
+        low = p * panel_rows
+        lanes = lax.broadcasted_iota(jnp.int32, (panel_rows, 2 * sk), 1)
+        lines = lax.broadcasted_iota(jnp.int32, (panel_rows, 2 * sk), 0)
+
+        def step(r, panel):
+            row = jnp.sum(jnp.where(lines == r, panel, 0.0), axis=0, keepdims=True)
+            column = jnp.sum(jnp.where(lanes[:, :sk] == low + r, panel[:, :sk], 0.0), axis=1, keepdims=True)
+            pivot = jnp.sum(jnp.where(lanes[0:1, :sk] == low + r, row[:, :sk], 0.0), axis=1, keepdims=True)
+            scale = lax.rsqrt(pivot)
+            row = row * scale
+            below = panel - (column * scale) * row
+            return jnp.where(lines < r, panel, jnp.where(lines == r, row, below))
+
+        panel = lax.fori_loop(0, panel_rows, step, work[low : low + panel_rows, :])
+        work[low : low + panel_rows, :] = panel
+        high = low + panel_rows
+        if high < sk:
+            update = lax.dot_general(
+                panel[:, :sk], panel, contract, precision=lax.Precision.HIGHEST, preferred_element_type=jnp.float32
+            )
+            work[high:, :] = work[high:, :] - update[high:, :]
+
+    eliminate(0)
     fourth(2)
-    second(0)
+    eliminate(1)
     fourth(1)
+    eliminate(2)
     fourth(3)
+    eliminate(3)
     total = third(0)
+    projected = lax.dot_general(zs[...], hid_ref[...], contract, preferred_element_type=jnp.float32)
+    sketch_ref[...] = jnp.dot(
+        work[:, sk:], projected, precision=lax.Precision.HIGHEST, preferred_element_type=jnp.float32
+    )
     for k in (2, 1, 3):
         z_copy(k).wait_recv()
         total = total + zr[k - 1].astype(jnp.float32)
     out_ref[...] = total.astype(out_ref.dtype)
-    for c in q:
+    for c in q[2:]:
         c.wait_send()
     for k in range(4):
         for j in range(4):
@@ -311,10 +368,11 @@
     spec = pl.BlockSpec(memory_space=pltpu.VMEM)
     return pl.pallas_call(
         combine_kernel,
-        out_shape=(jax.ShapeDtypeStruct((rows, cols), kind), jax.ShapeDtypeStruct((total, sk), kind)),
+        out_shape=(jax.ShapeDtypeStruct((rows, cols), kind), jax.ShapeDtypeStruct((sk, hidden.shape[1]), jnp.float32)),
         in_specs=[spec] * 4,
         out_specs=(spec, spec),
-        scratch_shapes=[vmem((4, 4, rows, cols), kind)] * 3
+        scratch_shapes=[vmem((sk, 2 * sk), jnp.float32)]
+        + [vmem((4, 4, rows, cols), kind)] * 3
         + [vmem((4, rows // 2, cols), kind)] * 2
         + [vmem((4, rows, cols), kind)] * 2
         + [vmem((3, rows, cols), kind)] * 2
@@ -331,18 +389,12 @@
     owners = lax.axis_size("expert")
     experts = jnp.arange(owners, dtype=jnp.int32)
     table = jnp.sum(jnp.where(routes[:, :, None] == experts, route_weights[:, :, None], 0.0), axis=1)
-    tables = lax.all_gather(table, "expert", axis=0, tiled=True)
-    features = gather_tokens(tokens)
+    features, tables = gather_tokens(tokens, table)
     weight = jnp.sum(jnp.where(experts == lax.axis_index("expert"), tables, 0.0), axis=1, keepdims=True)
     gate_val = jnp.dot(features, gate_weight[0], preferred_element_type=jnp.float32)
     up_val = jnp.dot(features, up_weight[0], preferred_element_type=jnp.float32)
     hidden = jnp.where(weight > 0, jax.nn.silu(gate_val) * up_val, 0.0).astype(jnp.bfloat16)
-    mixed, sketch_full = combine(hidden, down_weight[0], sketch_basis, weight, *tokens.shape)
-    contract = (((0,), (0,)), ((), ()))
-    gram = lax.dot_general(sketch_full, sketch_full, contract, preferred_element_type=jnp.float32)
-    lower_factor = jnp.linalg.cholesky(gram + ridge_term * jnp.eye(gram.shape[0], dtype=jnp.float32))
-    projected = lax.dot_general(sketch_full, hidden, contract, preferred_element_type=jnp.float32)
-    whitened = jax.scipy.linalg.solve_triangular(lower_factor, projected, lower=True)
+    mixed, whitened = combine(hidden, down_weight[0], sketch_basis, weight, *tokens.shape)
     return (mixed, whitened[None])
 
 

time: 172 us -> 143 us (0.83)
  other arithmetic: 23 us -> 2.11 us
  blocking collectives: 20.6 us -> 0 us
  Pallas kernels: 103 us -> 117 us
  matrix products: 22.2 us -> 18.3 us
  local copies, waits for them, and re-layouts: 2.8 us -> 5.05 us
    another operation x5 -> x0, other arithmetic: 22.9 us -> none  [the longest x3 12.4 us: dense_body(): jnp.linalg.cholesky(gram + ridge_term * jnp.eye(gram.shape[0], dtype=jnp....]
    all_gather x1 -> x0, blocking collectives: 20.6 us -> none  [dense_body(): tables = lax.all_gather(table, 'expert', axis=0, tiled=True)]
    pallas_call x1, Pallas kernels: 56.8 us -> 70.5 us  [combine(): pl.pallas_call(combine_kernel, out_shape=(jax.ShapeDtypeStruct((rows, col...]
    dot_general x2 -> x0, matrix products: 2.84 us -> none  [the longest x1 1.54 us: dense_body(): lax.dot_general(sketch_full, hidden, contract, preferred_element_type=jnp...]
where the time goes in v2:
time: 143 us
  Pallas kernels  117 us (82%)
  matrix products  18.3 us (13%)
  local copies, waits for them, and re-layouts  5.05 us (4%)
  other arithmetic  2.11 us (1%)
    pallas_call x1, Pallas kernels, combine(): pl.pallas_call(combine_kernel, out_shape=(jax.ShapeDtypeStruct((rows, col...  70.5 us
    pallas_call x1, Pallas kernels, gather_tokens(): pl.pallas_call(gather_kernel, out_shape=(jax.ShapeDtypeStruct((rows * 8,...  46 us
    dot_general x1, matrix products, dense_body(): up_val = jnp.dot(features, up_weight[0], preferred_element_type=jnp.float32)  10.2 us
    dot_general x1, matrix products, dense_body(): jnp.dot(features, gate_weight[0], preferred_element_type=jnp.float32)  8.1 us
    unnamed x4, local copies, waits for them, and re-layouts  3.29 us

profile of v2, /device:TPU:0, one launch (start us, length us, event | category | flops | bytes accessed | tf_op | source)
XLA Modules:
  0.0 142.7 jit_solution(14087912167225769306)
XLA Ops:
  0.6 0.0 copy-start
  0.6 0.9 select_reduce_fusion.1
  1.5 0.7 copy.14.tab_ref
  2.2 46.0 %shard_map.86 = (bf16[1024,4096]{1,0:T(8,128)(2,1)}, f32[1024,8]{1,0:T(8,128)}) custom-call(bf16[128,1024]{1,0:T(8,128)(2,1)} %tok_ref.1, f32[128,8]{1,0:T(8,128)} %copy.14.tab_ref), custom_call_target="tpu_custom_call" | custom-call | tf_op jit(solution)/shard_map/pallas_call | solution.py:187
  48.3 0.0 copy-done
  48.3 8.1 %fusion.2 = f32[1024,384]{1,0:T(8,128)} fusion(bf16[1024,4096]{1,0:T(8,128)(2,1)} %get-tuple-element.7, bf16[1,4096,384]{2,1,0:T(8,128)(2,1)S(1)} %copy-done), kind=kOutput, calls=%fused_computation.2 | convolution fusion | flops 3221225472 | bytes 13107200 | tf_op jit(solution)/shard_map/dot_general | solution.py:394
  56.4 1.2 select_reduce_fusion
  57.7 10.2 %select_convert_fusion.hid_ref = bf16[1024,384]{1,0:T(8,128)(2,1)} fusion(f32[1024,384]{1,0:T(8,128)} %fusion.2, bf16[1024,4096]{1,0:T(8,128)(2,1)} %get-tuple-element.7, bf16[1,4096,384]{2,1,0:T(8,128)(2,1)} %param.11, pred[1024]{0:T(1024)(128)(4,1)S(1)} %broadcast_compare_fusion), kind=kOutput, calls=%fused_computation.4 | convolution fusion | flops 3223977984 | bytes 13894656 | tf_op jit(solution)/shard_map/dot_general | solution.py:395
  67.9 1.0 copy.15.w_ref
  68.9 70.5 %shard_map.87 = (bf16[128,1024]{1,0:T(8,128)(2,1)}, f32[128,384]{1,0:T(8,128)}) custom-call(bf16[1024,384]{1,0:T(8,128)(2,1)} %select_convert_fusion.hid_ref, bf16[384,4096]{1,0:T(8,128)(2,1)} %bitcast.13, bf16[384,128]{1,0:T(8,128)(2,1)} %basis_ref.1, f32[1024,1]{1,0:T(8,128)} %copy.15.w_ref), custom_call_target="tpu_custom_call" | custom-call | tf_op jit(solution)/shard_map/pallas_call | solution.py:369
  139.4 1.7 %copy.18 = bf16[128,1024]{1,0:T(8,128)(2,1)} copy(bf16[128,1024]{1,0:T(8,128)(2,1)} %get-tuple-element.12) | data formatting | bytes 524288
  141.1 1.6 %copy.19 = f32[1,128,384]{2,1,0:T(8,128)} copy(f32[1,128,384]{2,1,0:T(8,128)} %bitcast.14) | data formatting | bytes 393216
  (2 shorter events, 0.0 us)
Async XLA Ops:
  0.6 47.7 %copy-start = (bf16[1,4096,384]{2,1,0:T(8,128)(2,1)S(1)}, bf16[1,4096,384]{2,1,0:T(8,128)(2,1)}, u32[]{:S(2)}) copy-start(bf16[1,4096,384]{2,1,0:T(8,128)(2,1)} %param.10) | copy-start | bytes 9437188

commit v3 on v2

--- a/solution.py
+++ b/solution.py
@@ -91,7 +91,7 @@
     pl.semaphore_wait(barrier, len(partners))
 
 
-def gather_kernel(tok_ref, tab_ref, out_ref, tabs_ref, own_sem, tab_sem, t_send, t_recv, z_send, z_recv, x_send, x_recv, y_send, y_recv, dx_send, dx_recv, dy_send, dy_recv, s_send, s_recv):
+def hidden_kernel(tok_ref, tab_ref, gate_ref, up_ref, hid_ref, w_ref, out_ref, tabs_ref, gate_w, up_w, gate_acc, up_acc, gw_sem, uw_sem, own_sem, tab_sem, t_send, t_recv, z_send, z_recv, x_send, x_recv, y_send, y_recv, dx_send, dx_recv, dy_send, dy_recv, s_send, s_recv):
     dp, expert, y, x, z, core = place()
     rows, cols = tok_ref.shape
     half = rows // 2
@@ -111,6 +111,7 @@
             src_ref=ref, dst_ref=dst, send_sem=send, recv_sem=recv, device_id=device, device_id_type=MESH
         )
 
+    weights = (pltpu.make_async_copy(gate_ref, gate_w, gw_sem), pltpu.make_async_copy(up_ref, up_w, uw_sem))
     sent = []
 
     def go(*args):
@@ -156,45 +157,97 @@
         go(block(dp, k), block(dp, k), y_send.at[k], y_recv.at[k], y_dev)
         go(block(dp, k), block(dp, k), s_send.at[k], s_recv.at[k], other)
 
+    for c in weights:
+        c.start()
+    columns_of = (dp, x_dp, y_dp, d_dp)
+
+    def pair(j, k):
+        at = ((z + 4 - k) % 4 * 2 + 1 - core) * rows
+        col = pl.multiple_of(columns_of[j] * cols, cols)
+        arrived(out_ref.at[pl.ds(at, rows), pl.ds(col, cols)], s_send.at[4 * j + k], s_recv.at[4 * j + k])
+        both = pl.ds(pl.multiple_of((z + 4 - k) % 4 * 2 * rows, 2 * rows), 2 * rows)
+        piece = out_ref[both, pl.ds(col, cols)]
+        for acc, matrix in ((gate_acc, gate_w), (up_acc, up_w)):
+            value = jnp.dot(piece, matrix[pl.ds(col, cols), :], preferred_element_type=jnp.float32)
+            acc[both, :] = value if j == 0 else acc[both, :] + value
+
+    def finish(k):
+        both = pl.ds(pl.multiple_of((z + 4 - k) % 4 * 2 * rows, 2 * rows), 2 * rows)
+        gate = gate_acc[both, :]
+        value = gate / (1.0 + jnp.exp(-gate)) * up_acc[both, :]
+        hid_ref[both, :] = jnp.where(w_ref[both, :] > 0, value, 0.0).astype(hid_ref.dtype)
+
     column(1)
     near(0)
     column(3)
+    own.wait()
+    for c in weights:
+        c.wait()
+    pair(0, 0)
     column(2)
+    pair(1, 0)
+    pair(2, 0)
+    pair(0, 1)
     near(1)
     far(0)
-    near(3)
-    far(1)
-    near(2)
-    far(3)
-    far(2)
-    for j, dp_at in enumerate((dp, x_dp, y_dp, d_dp)):
-        for k in range(4):
-            at = ((z + 4 - k) % 4 * 2 + 1 - core) * rows
-            dst = out_ref.at[pl.ds(at, rows), pl.ds(dp_at * cols, cols)]
-            arrived(dst, s_send.at[4 * j + k], s_recv.at[4 * j + k])
+    own_tab.wait()
     for i in range(7):
         k, side = (0, 1 - core) if i == 0 else (i, core) if i < 4 else (i - 3, 1 - core)
         arrived(table_at(k, side), t_send.at[i], t_recv.at[i])
-    own.wait()
-    own_tab.wait()
+    experts = lax.broadcasted_iota(jnp.int32, tabs_ref.shape, 1)
+    w_ref[...] = jnp.sum(jnp.where(experts == expert, tabs_ref[...], 0.0), axis=1, keepdims=True)
+    pair(0, 3)
+    pair(0, 2)
+    near(3)
+    far(1)
+    pair(3, 0)
+    finish(0)
+    pair(1, 1)
+    pair(2, 1)
+    near(2)
+    far(3)
+    pair(3, 1)
+    finish(1)
+    pair(1, 3)
+    pair(2, 3)
+    far(2)
+    pair(3, 3)
+    finish(3)
+    pair(1, 2)
+    pair(2, 2)
+    pair(3, 2)
+    finish(2)
     for c in sent:
         c.wait_send()
 
 
-def gather_tokens(tokens, table):
+def hidden_units(tokens, table, gate, up):
     rows, cols = tokens.shape
-    dma = pltpu.SemaphoreType.DMA
+    dma, vmem = pltpu.SemaphoreType.DMA, pltpu.VMEM
+    units = gate.shape[1]
     return pl.pallas_call(
-        gather_kernel,
+        hidden_kernel,
         out_shape=(
-            jax.ShapeDtypeStruct((rows * 8, cols * 4), tokens.dtype),
-            jax.ShapeDtypeStruct((rows * 8, table.shape[1]), table.dtype),
+            jax.ShapeDtypeStruct((rows * 8, units), tokens.dtype),
+            jax.ShapeDtypeStruct((rows * 8, 1), table.dtype),
         ),
-        in_specs=[pl.BlockSpec(memory_space=pl.ANY)] * 2,
-        out_specs=(pl.BlockSpec(memory_space=pl.ANY),) * 2,
-        scratch_shapes=[dma, dma, dma((7,)), dma((7,)), dma((3,)), dma((3,))] + [dma((4,))] * 8 + [dma((16,))] * 2,
+        in_specs=[pl.BlockSpec(memory_space=pltpu.VMEM)] * 2 + [pl.BlockSpec(memory_space=pl.ANY)] * 2,
+        out_specs=(pl.BlockSpec(memory_space=pltpu.VMEM),) * 2,
+        scratch_shapes=[
+            vmem((rows * 8, cols * 4), tokens.dtype),
+            vmem((rows * 8, table.shape[1]), table.dtype),
+            vmem(gate.shape, gate.dtype),
+            vmem(up.shape, up.dtype),
+            vmem((rows * 8, units), jnp.float32),
+            vmem((rows * 8, units), jnp.float32),
+        ]
+        + [dma] * 4
+        + [dma((7,))] * 2
+        + [dma((3,))] * 2
+        + [dma((4,))] * 8
+        + [dma((16,))] * 2,
         compiler_params=pltpu.CompilerParams(collective_id=0, has_side_effects=True, vmem_limit_bytes=VMEM_BYTES),
-    )(tokens, table)
+    )(tokens, table, gate, up)
 
 
 def combine_kernel(hid_ref, down_ref, basis_ref, w_ref, out_ref, sketch_ref, work, sbuf, rbuf, pbuf, dxb, dyb, xb, yb, zb, zr, zs, zn, z2, zz,
@@ -254,27 +307,29 @@
         return copy(zb.at[k - 1], zr.at[k - 1], z_send.at[k - 1], z_recv.at[k - 1], z_devs[k - 1])
 
     order = (2, 1, 3, 0)
-    for k in order:
-        for j in (3, 1, 2, 0):
-            sbuf[k, j] = product(k, j, 1 - core).astype(sbuf.dtype)
-            s_copy(k, j).start()
+
+    def give(k, j):
+        sbuf[k, j] = product(k, j, 1 - core).astype(sbuf.dtype)
+        s_copy(k, j).start()
+
+    def own(k, j):
+        mine = product(k, j, core)
+        s_copy(k, j).wait_recv()
+        pbuf[k, j] = (mine + rbuf[k, j].astype(jnp.float32)).astype(pbuf.dtype)
+
+    for k in order:
+        give(k, 3)
+    for k in order:
+        own(k, 3)
+        dx_copy(k).start()
+        dy_copy(k).start()
+    for k in order:
+        give(k, 2)
+        give(k, 1)
     for i, part in ((0, lo), (1, hi)):
         q[i].wait_recv()
         z2[part, :] = (zs[part, :].astype(jnp.float32) + zn[part, :].astype(jnp.float32)).astype(z2.dtype)
         q[2 + i].start()
-
-    def own(k, j):
-        mine = product(k, j, core)
-        s_copy(k, j).wait_recv()
-        pbuf[k, j] = (mine + rbuf[k, j].astype(jnp.float32)).astype(pbuf.dtype)
-
-    def first(k):
-        own(k, 3)
-        dx_copy(k).start()
-        dy_copy(k).start()
-        own(k, 1)
-        own(k, 2)
-        own(k, 0)
 
     def second(k):
         dx_copy(k).wait_recv()
@@ -294,16 +349,18 @@
         z_copy(k).start()
 
     for k in order:
-        first(k)
+        own(k, 2)
+        own(k, 1)
+        second(k)
+    for k in order:
+        give(k, 0)
+    for k in order:
+        own(k, 0)
     q[2].wait_recv()
     q[3].wait_recv()
     q[0].wait_send()
     q[1].wait_send()
     zs[...] = (z2[...].astype(jnp.float32) + zz[...].astype(jnp.float32)).astype(zs.dtype)
-    second(2)
-    second(1)
-    second(3)
-    second(0)
     sk = work.shape[0]
     panel_rows = 32
     contract = (((0,), (0,)), ((), ()))
@@ -389,11 +446,7 @@
     owners = lax.axis_size("expert")
     experts = jnp.arange(owners, dtype=jnp.int32)
     table = jnp.sum(jnp.where(routes[:, :, None] == experts, route_weights[:, :, None], 0.0), axis=1)
-    features, tables = gather_tokens(tokens, table)
-    weight = jnp.sum(jnp.where(experts == lax.axis_index("expert"), tables, 0.0), axis=1, keepdims=True)
-    gate_val = jnp.dot(features, gate_weight[0], preferred_element_type=jnp.float32)
-    up_val = jnp.dot(features, up_weight[0], preferred_element_type=jnp.float32)
-    hidden = jnp.where(weight > 0, jax.nn.silu(gate_val) * up_val, 0.0).astype(jnp.bfloat16)
+    hidden, weight = hidden_units(tokens, table, gate_weight[0], up_weight[0])
     mixed, whitened = combine(hidden, down_weight[0], sketch_basis, weight, *tokens.shape)
     return (mixed, whitened[None])
 

time: 143 us -> 123 us (0.86)
  matrix products: 18.3 us -> 0 us
    dot_general x2 -> x0, matrix products: 18.3 us -> none  [the longest x1 10.2 us: dense_body(): up_val = jnp.dot(features, up_weight[0], preferred_element_type=jnp.float32)]
    pallas_call x1, Pallas kernels: 46 us -> 54.6 us  [hidden_units(): pl.pallas_call(hidden_kernel, out_shape=(jax.ShapeDtypeStruct((rows * 8,...]
    pallas_call x1, Pallas kernels: 70.5 us -> 62.6 us  [combine(): pl.pallas_call(combine_kernel, out_shape=(jax.ShapeDtypeStruct((rows, col...]
    unnamed x4 -> x2, local copies, waits for them, and re-layouts: 3.29 us -> 3.29 us
where the time goes in v3:
time: 123 us
  Pallas kernels  117 us (95%)
  local copies, waits for them, and re-layouts  4.02 us (3%)
    pallas_call x1, Pallas kernels, combine(): pl.pallas_call(combine_kernel, out_shape=(jax.ShapeDtypeStruct((rows, col...  62.6 us
    pallas_call x1, Pallas kernels, hidden_units(): pl.pallas_call(hidden_kernel, out_shape=(jax.ShapeDtypeStruct((rows * 8,...  54.6 us
    unnamed x2, local copies, waits for them, and re-layouts  3.29 us

profile of v3, /device:TPU:0, one launch (start us, length us, event | category | flops | bytes accessed | tf_op | source)
XLA Modules:
  0.0 122.6 jit_solution(15581510777291950768)
XLA Ops:
  0.6 0.7 select_reduce_fusion
  1.3 0.7 copy.11.tab_ref
  2.1 54.6 %shard_map.86 = (bf16[1024,384]{1,0:T(8,128)(2,1)}, f32[1024,1]{1,0:T(8,128)}) custom-call(bf16[128,1024]{1,0:T(8,128)(2,1)} %tok_ref.1, f32[128,8]{1,0:T(8,128)} %copy.11.tab_ref, bf16[4096,384]{1,0:T(8,128)(2,1)} %bitcast.4, bf16[4096,384]{1,0:T(8,128)(2,1)} %bitcast.5), custom_call_target="tpu_custom_call" | custom-call | tf_op jit(solution)/shard_map/pallas_call | solution.py:228
  56.7 62.6 %shard_map.87 = (bf16[128,1024]{1,0:T(8,128)(2,1)}, f32[128,384]{1,0:T(8,128)}) custom-call(bf16[1024,384]{1,0:T(8,128)(2,1)} %get-tuple-element.6.hid_ref, bf16[384,4096]{1,0:T(8,128)(2,1)} %bitcast.6, bf16[384,128]{1,0:T(8,128)(2,1)} %basis_ref.1, f32[1024,1]{1,0:T(8,128)} %get-tuple-element.7.w_ref), custom_call_target="tpu_custom_call" | custom-call | tf_op jit(solution)/shard_map/pallas_call | solution.py:426
  119.3 1.7 %copy.14 = bf16[128,1024]{1,0:T(8,128)(2,1)} copy(bf16[128,1024]{1,0:T(8,128)(2,1)} %get-tuple-element.12) | data formatting | bytes 524288
  121.0 1.6 %copy.15 = f32[1,128,384]{2,1,0:T(8,128)} copy(f32[1,128,384]{2,1,0:T(8,128)} %bitcast.7) | data formatting | bytes 393216

commit v4 on v3

--- a/solution.py
+++ b/solution.py
@@ -392,12 +392,12 @@
             )
             work[high:, :] = work[high:, :] - update[high:, :]
 
+    fourth(2)
     eliminate(0)
-    fourth(2)
+    fourth(1)
     eliminate(1)
-    fourth(1)
+    fourth(3)
     eliminate(2)
-    fourth(3)
     eliminate(3)
     total = third(0)
     projected = lax.dot_general(zs[...], hid_ref[...], contract, preferred_element_type=jnp.float32)

time: 123 us -> 123 us (level)
  no operation moved by 1% of the time
where the time goes in v4:
time: 123 us
  Pallas kernels  117 us (95%)
  local copies, waits for them, and re-layouts  4.02 us (3%)
    pallas_call x1, Pallas kernels, combine(): pl.pallas_call(combine_kernel, out_shape=(jax.ShapeDtypeStruct((rows, col...  62.6 us
    pallas_call x1, Pallas kernels, hidden_units(): pl.pallas_call(hidden_kernel, out_shape=(jax.ShapeDtypeStruct((rows * 8,...  54.6 us
    unnamed x2, local copies, waits for them, and re-layouts  3.29 us

profile of v4, /device:TPU:0, one launch (start us, length us, event | category | flops | bytes accessed | tf_op | source)
XLA Modules:
  0.0 122.6 jit_solution(16864614113986945943)
XLA Ops:
  0.6 0.7 select_reduce_fusion
  1.3 0.7 copy.11.tab_ref
  2.1 54.6 %shard_map.86 = (bf16[1024,384]{1,0:T(8,128)(2,1)}, f32[1024,1]{1,0:T(8,128)}) custom-call(bf16[128,1024]{1,0:T(8,128)(2,1)} %tok_ref.1, f32[128,8]{1,0:T(8,128)} %copy.11.tab_ref, bf16[4096,384]{1,0:T(8,128)(2,1)} %bitcast.4, bf16[4096,384]{1,0:T(8,128)(2,1)} %bitcast.5), custom_call_target="tpu_custom_call" | custom-call | tf_op jit(solution)/shard_map/pallas_call | solution.py:228
  56.7 62.6 %shard_map.87 = (bf16[128,1024]{1,0:T(8,128)(2,1)}, f32[128,384]{1,0:T(8,128)}) custom-call(bf16[1024,384]{1,0:T(8,128)(2,1)} %get-tuple-element.6.hid_ref, bf16[384,4096]{1,0:T(8,128)(2,1)} %bitcast.6, bf16[384,128]{1,0:T(8,128)(2,1)} %basis_ref.1, f32[1024,1]{1,0:T(8,128)} %get-tuple-element.7.w_ref), custom_call_target="tpu_custom_call" | custom-call | tf_op jit(solution)/shard_map/pallas_call | solution.py:426
  119.3 1.7 %copy.14 = bf16[128,1024]{1,0:T(8,128)(2,1)} copy(bf16[128,1024]{1,0:T(8,128)(2,1)} %get-tuple-element.12) | data formatting | bytes 524288
  121.0 1.6 %copy.15 = f32[1,128,384]{2,1,0:T(8,128)} copy(f32[1,128,384]{2,1,0:T(8,128)} %bitcast.7) | data formatting | bytes 393216
